TPU v7x, 32 devices: a whole 2x2x4 slice. The times are simulated.
32 devices in a mesh: depth: 4 (over x, core), row: 4 (over z), col: 2 (over y).
Axes of the slice: x: 2, y: 2, z: 4, core: 2. Of those that a mesh axis runs over, the one named last changes fastest.
Arguments:
- density: float32 [4096, 4096], P('row', ('depth', 'col')), as said below
- pattern: int32 [64, 64], replicated, may hold values from 0 to 1, as said below
- filters: int32 [4, 64, 64], replicated, may hold values from 0 to 1, as said below
Outputs:
- purified: float32 [4096, 4096], P('row', ('depth', 'col'))
Inputs may be any that keep to these rules, and one draw needn't show every extreme that they name: density is symmetric. `pattern`: symmetric 0/1 block table with every diagonal block set. `filters`: each table is a symmetric 0/1 block table with every diagonal block set.
All inputs are finite; a program needn't handle non-finite values.
Results may differ from a plain program's by a relative error of at most 0.007.
Values may be sent and summed in bfloat16 or wider, within the bound.
A program may use at most 64 MiB of HBM per device.

v0:
```python
import jax
import jax.numpy as jnp
from jax import lax
from jax.sharding import PartitionSpec as P

BLK = 64
PURIFY = 2


def spread(value, axis, root):
    mine = lax.axis_index(axis) == root
    return lax.psum(jnp.where(mine, value, jnp.zeros_like(value)), axis)


def on_device(density, pattern, filters):
    rows_wide, seg_width = density.shape
    n_depth = lax.axis_size("depth")
    n_col = lax.axis_size("col")
    layer_index = lax.axis_index("depth")
    row_index = lax.axis_index("row")
    col_index = lax.axis_index("col")
    row_blocks = rows_wide // BLK
    seg_blocks = seg_width // BLK

    def full_mask(keep_table):
        row_strip = lax.dynamic_slice_in_dim(keep_table, row_index * row_blocks, row_blocks, 0)
        groups = row_strip.reshape(row_blocks, n_depth, n_col, seg_blocks)
        picked = lax.dynamic_slice_in_dim(groups, col_index, 1, 2)
        return picked.reshape(row_blocks, n_depth * seg_blocks).astype(jnp.float32)

    def own_mask(keep_table):
        return lax.dynamic_slice_in_dim(
            full_mask(keep_table), layer_index * seg_blocks, seg_blocks, 1
        )

    def apply_mask(values, keep_mask):
        row_count, col_count = keep_mask.shape
        shaped = values.reshape(row_count, BLK, col_count, BLK) * keep_mask[:, None, :, None]
        return shaped.reshape(values.shape)

    def multiply(left_tile, right_side):
        return jnp.dot(
            lax.all_gather(left_tile, "col", axis=1, tiled=True),
            right_side,
            preferred_element_type=jnp.float32,
        )

    def share_layers(partial_sum):
        return lax.psum_scatter(partial_sum, "depth", scatter_dimension=1, tiled=True)

    start_matrix = apply_mask(density, own_mask(pattern))
    current = start_matrix
    for round_index in range(PURIFY):
        operand = current.astype(jnp.bfloat16)
        right_side = spread(
            lax.all_gather(operand, "depth", axis=1, tiled=True), "row", layer_index
        )
        square = apply_mask(
            share_layers(multiply(operand, right_side)), own_mask(filters[2 * round_index])
        )
        cubic = apply_mask(
            share_layers(multiply(square.astype(jnp.bfloat16), right_side)),
            own_mask(filters[2 * round_index + 1]),
        )
        current = 3.0 * square - 2.0 * cubic
    return current


def solution(mesh):
    return jax.shard_map(
        on_device,
        mesh=mesh,
        in_specs=(P("row", ("depth", "col")), P(), P()),
        out_specs=P("row", ("depth", "col")),
        check_vma=False,
    )
```

profile of v0, /device:TPU:0, one launch (start us, length us, event | category | flops | bytes accessed | tf_op | source)
XLA Modules:
  0.0 889.9 jit_solution(13428316623293829066)
XLA Ops:
  6.5 0.8 copy-done
  7.3 0.1 copy.14
  7.4 0.1 copy.5
  7.5 2.3 mul.83
  9.8 3.4 mul.84
  13.2 2.9 multiply_convert_fusion
  16.1 0.0 all-gather.7.cloned.1.call-start
  16.2 0.7 all-gather.7.cloned.1.call-update
  16.9 0.0 all-reduce.3.cloned.1.call-start
  16.9 36.5 %all-gather.9.cloned.1.call-done = bf16[1024,2048]{1,0:T(8,128)(2,1)} async-done(((bf16[1024,512]{1,0:T(8,128)(2,1)}), bf16[1024,2048]{1,0:T(8,128)(2,1)}) %all-gather.9.cloned.1.call-update) | async-done | bytes 4194320 | tf_op jit(solution)/shard_map/all_gather | solution.py:56
  53.5 4.5 broadcast_select_fusion.1
  57.9 0.0 all-reduce.3.cloned.1.call-update
  57.9 0.0 reduce-scatter.5.cloned.1.call-start
  58.0 30.2 %all-gather.7.cloned.1.call-done = bf16[1024,1024]{1,0:T(8,128)(2,1)} async-done(((bf16[1024,512]{1,0:T(8,128)(2,1)}), bf16[1024,1024]{1,0:T(8,128)(2,1)}) %all-gather.7.cloned.1.call-update) | async-done | bytes 2097168 | tf_op jit(solution)/shard_map/all_gather | solution.py:43
  88.2 157.4 %all-reduce.3.cloned.1.call-done = bf16[1024,2048]{1,0:T(8,128)(2,1)} async-done(((bf16[1024,2048]{1,0:T(8,128)(2,1)}), bf16[1024,2048]{1,0:T(8,128)(2,1)}) %all-reduce.3.cloned.1.call-update) | async-done | bytes 4194320 | tf_op jit(solution)/shard_map/psum | solution.py:12
  245.5 10.6 %fusion.1 = f32[1024,2048]{1,0:T(8,128)} fusion(bf16[1024,1024]{1,0:T(8,128)(2,1)} %all-gather.7.cloned.1.call-done, bf16[1024,2048]{1,0:T(8,128)(2,1)} %all-reduce.3.cloned.1.call-done), kind=kOutput, calls=%fused_computation.23 | convolution fusion | flops 4294967296 | bytes 14680064 | tf_op jit(solution)/shard_map/dot_general | solution.py:42
  256.1 0.0 reduce-scatter.5.cloned.1.call-update
  256.1 0.0 all-gather.11.cloned.1.call-start
  256.2 0.8 copy-done.2
  257.0 0.1 copy.16
  257.1 0.1 copy.7
  257.2 2.3 mul.86
  259.5 3.8 mul.87
  263.3 63.7 %reduce-scatter.5.cloned.1.call-done = f32[1024,512]{1,0:T(8,128)} async-done(((f32[1024,2048]{1,0:T(8,128)}), f32[1024,512]{1,0:T(8,128)}) %reduce-scatter.5.cloned.1.call-update) | async-done | bytes 2097168 | tf_op jit(solution)/shard_map/reduce_scatter | solution.py:49
  327.0 2.9 multiply_convert_fusion.2
  329.9 0.0 all-gather.11.cloned.1.call-update
  329.9 0.0 reduce-scatter.7.cloned.1.call-start
  330.0 33.2 %all-gather.11.cloned.1.call-done = bf16[1024,1024]{1,0:T(8,128)(2,1)} async-done(((bf16[1024,512]{1,0:T(8,128)(2,1)}), bf16[1024,1024]{1,0:T(8,128)(2,1)}) %all-gather.11.cloned.1.call-update) | async-done | bytes 2097168 | tf_op jit(solution)/shard_map/all_gather | solution.py:43
  363.2 10.6 %fusion.2 = f32[1024,2048]{1,0:T(8,128)} fusion(bf16[1024,1024]{1,0:T(8,128)(2,1)} %all-gather.11.cloned.1.call-done, bf16[1024,2048]{1,0:T(8,128)(2,1)} %all-reduce.3.cloned.1.call-done), kind=kOutput, calls=%fused_computation.24 | convolution fusion | flops 4294967296 | bytes 14680064 | tf_op jit(solution)/shard_map/dot_general | solution.py:42
  373.8 0.0 reduce-scatter.7.cloned.1.call-update
  373.8 0.2 all-gather.15.cloned.1.call-start
  374.1 0.1 copy.18
  374.2 0.1 copy.9
  374.2 2.3 mul.90
  376.6 5.0 mul.91
  381.6 64.1 %reduce-scatter.7.cloned.1.call-done = f32[1024,512]{1,0:T(8,128)} async-done(((f32[1024,2048]{1,0:T(8,128)}), f32[1024,512]{1,0:T(8,128)}) %reduce-scatter.7.cloned.1.call-update) | async-done | bytes 2097168 | tf_op jit(solution)/shard_map/reduce_scatter | solution.py:49
  445.7 4.9 subtract_convert_fusion
  450.7 0.0 all-gather.15.cloned.1.call-update
  450.7 0.0 all-gather.13.cloned.1.call-start
  450.7 0.7 all-gather.13.cloned.1.call-update
  451.4 0.0 all-reduce.5.cloned.1.call-start
  451.5 33.8 %all-gather.15.cloned.1.call-done = bf16[1024,2048]{1,0:T(8,128)(2,1)} async-done(((bf16[1024,512]{1,0:T(8,128)(2,1)}), bf16[1024,2048]{1,0:T(8,128)(2,1)}) %all-gather.15.cloned.1.call-update) | async-done | bytes 4194320 | tf_op jit(solution)/shard_map/all_gather | solution.py:56
  485.3 4.4 broadcast_select_fusion
  489.7 0.0 all-reduce.5.cloned.1.call-update
  489.8 0.0 reduce-scatter.9.cloned.1.call-start
  489.8 30.3 %all-gather.13.cloned.1.call-done = bf16[1024,1024]{1,0:T(8,128)(2,1)} async-done(((bf16[1024,512]{1,0:T(8,128)(2,1)}), bf16[1024,1024]{1,0:T(8,128)(2,1)}) %all-gather.13.cloned.1.call-update) | async-done | bytes 2097168 | tf_op jit(solution)/shard_map/all_gather | solution.py:43
  520.1 157.5 %all-reduce.5.cloned.1.call-done = bf16[1024,2048]{1,0:T(8,128)(2,1)} async-done(((bf16[1024,2048]{1,0:T(8,128)(2,1)}), bf16[1024,2048]{1,0:T(8,128)(2,1)}) %all-reduce.5.cloned.1.call-update) | async-done | bytes 4194320 | tf_op jit(solution)/shard_map/psum | solution.py:12
  677.6 10.6 %fusion.3 = f32[1024,2048]{1,0:T(8,128)} fusion(bf16[1024,1024]{1,0:T(8,128)(2,1)} %all-gather.13.cloned.1.call-done, bf16[1024,2048]{1,0:T(8,128)(2,1)} %all-reduce.5.cloned.1.call-done), kind=kOutput, calls=%fused_computation.25 | convolution fusion | flops 4294967296 | bytes 14680064 | tf_op jit(solution)/shard_map/dot_general | solution.py:42
  688.2 0.0 all-gather.17.cloned.1.call-start
  688.3 0.1 copy.20
  688.4 0.1 copy.11
  688.5 2.3 mul.94
  690.7 3.5 mul.95
  694.3 64.9 %reduce-scatter.9.cloned.1.call-done = f32[1024,512]{1,0:T(8,128)} async-done(((f32[1024,2048]{1,0:T(8,128)}), f32[1024,512]{1,0:T(8,128)}) %reduce-scatter.9.cloned.1.call-update) | async-done | bytes 2097168 | tf_op jit(solution)/shard_map/reduce_scatter | solution.py:49
  759.1 2.9 multiply_convert_fusion.1
  762.1 0.3 reduce-scatter.11.cloned.1.call-start
  762.3 33.0 %all-gather.17.cloned.1.call-done = bf16[1024,1024]{1,0:T(8,128)(2,1)} async-done(((bf16[1024,512]{1,0:T(8,128)(2,1)}), bf16[1024,1024]{1,0:T(8,128)(2,1)}) %all-gather.17.cloned.1.call-update) | async-done | bytes 2097168 | tf_op jit(solution)/shard_map/all_gather | solution.py:43
  795.3 10.6 %fusion.4 = f32[1024,2048]{1,0:T(8,128)} fusion(bf16[1024,1024]{1,0:T(8,128)(2,1)} %all-gather.17.cloned.1.call-done, bf16[1024,2048]{1,0:T(8,128)(2,1)} %all-reduce.5.cloned.1.call-done), kind=kOutput, calls=%fused_computation.26 | convolution fusion | flops 4294967296 | bytes 14680064 | tf_op jit(solution)/shard_map/dot_general | solution.py:42
  805.9 0.1 copy.22
  806.0 0.1 copy.13
  806.1 2.3 mul.98
  808.4 5.0 mul.99
  813.4 64.4 %reduce-scatter.11.cloned.1.call-done = f32[1024,512]{1,0:T(8,128)} async-done(((f32[1024,2048]{1,0:T(8,128)}), f32[1024,512]{1,0:T(8,128)}) %reduce-scatter.11.cloned.1.call-update) | async-done | bytes 2097168 | tf_op jit(solution)/shard_map/reduce_scatter | solution.py:49
  877.8 5.2 multiply_subtract_fusion
  (23 shorter events, 0.2 us)
Async XLA Ops:
  6.5 0.8 copy-start
  6.5 46.9 %all-gather.9.cloned.1.call-start = ((), (), s32[]{:S(2)}) async-start(), calls=%async_computation.5 | async-start | bytes 5242880 | tf_op jit(solution)/shard_map/all_gather | solution.py:56
  16.1 72.0 %all-gather.7.cloned.1.call-start = ((), (), s32[]{:S(2)}) async-start(), calls=%async_computation.4 | async-start | bytes 3145728 | tf_op jit(solution)/shard_map/all_gather | solution.py:43
  16.9 228.7 %all-reduce.3.cloned.1.call-start = ((), (), s32[]{:S(2)}) async-start(), calls=%async_computation.6 | async-start | bytes 8388608 | tf_op jit(solution)/shard_map/psum | solution.py:12
  57.9 269.1 %reduce-scatter.5.cloned.1.call-start = ((), (), s32[]{:S(2)}) async-start(), calls=%async_computation.7 | async-start | bytes 10485760 | tf_op jit(solution)/shard_map/reduce_scatter | solution.py:49
  256.1 0.9 copy-start.2
  256.1 107.1 %all-gather.11.cloned.1.call-start = ((), (), s32[]{:S(2)}) async-start(), calls=%async_computation.8 | async-start | bytes 3145728 | tf_op jit(solution)/shard_map/all_gather | solution.py:43
  329.9 115.8 %reduce-scatter.7.cloned.1.call-start = ((), (), s32[]{:S(2)}) async-start(), calls=%async_computation.9 | async-start | bytes 10485760 | tf_op jit(solution)/shard_map/reduce_scatter | solution.py:49
  373.8 111.5 %all-gather.15.cloned.1.call-start = ((), (), s32[]{:S(2)}) async-start(), calls=%async_computation.11 | async-start | bytes 5242880 | tf_op jit(solution)/shard_map/all_gather | solution.py:56
  450.7 69.4 %all-gather.13.cloned.1.call-start = ((), (), s32[]{:S(2)}) async-start(), calls=%async_computation.10 | async-start | bytes 3145728 | tf_op jit(solution)/shard_map/all_gather | solution.py:43
  451.4 226.2 %all-reduce.5.cloned.1.call-start = ((), (), s32[]{:S(2)}) async-start(), calls=%async_computation.12 | async-start | bytes 8388608 | tf_op jit(solution)/shard_map/psum | solution.py:12
  489.8 269.4 %reduce-scatter.9.cloned.1.call-start = ((), (), s32[]{:S(2)}) async-start(), calls=%async_computation.13 | async-start | bytes 10485760 | tf_op jit(solution)/shard_map/reduce_scatter | solution.py:49
  688.2 107.1 %all-gather.17.cloned.1.call-start = ((), (), s32[]{:S(2)}) async-start(), calls=%async_computation.14 | async-start | bytes 3145728 | tf_op jit(solution)/shard_map/all_gather | solution.py:43
  762.1 115.8 %reduce-scatter.11.cloned.1.call-start = ((), (), s32[]{:S(2)}) async-start(), calls=%async_computation.15 | async-start | bytes 10485760 | tf_op jit(solution)/shard_map/reduce_scatter | solution.py:49
  877.8 5.2 copy-start.1
Sparse Core Ops, SparseCore 0:
  16.2 37.1 all-gather.8
  55.0 33.1 all-gather.6
  90.5 154.9 all-reduce.2
  256.3 70.7 reduce-scatter.4
  330.1 33.1 all-gather.10
  373.9 71.7 reduce-scatter.6
  450.8 34.4 all-gather.14
  486.9 33.1 all-gather.12
  522.6 154.9 all-reduce.4
  688.3 70.7 reduce-scatter.8
  762.2 33.1 all-gather.16
  806.1 71.7 reduce-scatter.10
where the time goes:
time: 891 us; the launch traced here: 890 us
  waiting for transfers between devices  771 us (87%)
  matrix products  42.3 us (5%)
  local copies, waits for them, and re-layouts  34.7 us (4%)
  other arithmetic  27.8 us (3%)
  between operations  13.7 us (2%)
    psum x2, waiting for transfers between devices, spread(): return lax.psum(jnp.where(mine, value, jnp.zeros_like(value)), axis)  315 us
    reduce_scatter x4, waiting for transfers between devices, share_layers(): lax.psum_scatter(partial_sum, 'depth', scatter_dimension=1, tiled=True)  257 us
    all_gather x4, waiting for transfers between devices, multiply(): lax.all_gather(left_tile, 'col', axis=1, tiled=True)  127 us
    all_gather x2, waiting for transfers between devices, on_device(): lax.all_gather(operand, 'depth', axis=1, tiled=True)  70.4 us
    dot_general x4, matrix products, multiply(): jnp.dot(lax.all_gather(left_tile, 'col', axis=1, tiled=True), right_side,...  42.3 us
    mul x10, local copies, waits for them, and re-layouts, apply_mask(): values.reshape(row_count, BLK, col_count, BLK) * keep_mask[:, None, :, None]  32.3 us
  transfers between devices with their start and end apart: 12, of which 12 were waited for; matrix products, arithmetic and copies ran while one was open for 4% of the time, Pallas kernels for 0%

commit v1 on v0

--- a/solution.py
+++ b/solution.py
@@ -5,6 +5,18 @@
 
 BLK = 64
 PURIFY = 2
+
+
+def collect(array, axis, dim):
+    ways, here = (lax.axis_size(axis), lax.axis_index(axis))
+    grown, reach = (array, 1)
+    while reach < ways:
+        theirs = lax.ppermute(grown, axis, [(d, d ^ reach) for d in range(ways)])
+        mine_first = jnp.concatenate([grown, theirs], axis=dim)
+        theirs_first = jnp.concatenate([theirs, grown], axis=dim)
+        grown = jnp.where(here & reach == 0, mine_first, theirs_first)
+        reach = 2 * reach
+    return grown
 
 
 def spread(value, axis, root):
@@ -52,9 +64,7 @@
     current = start_matrix
     for round_index in range(PURIFY):
         operand = current.astype(jnp.bfloat16)
-        right_side = spread(
-            lax.all_gather(operand, "depth", axis=1, tiled=True), "row", layer_index
-        )
+        right_side = spread(collect(operand, "depth", 1), "row", layer_index)
         square = apply_mask(
             share_layers(multiply(operand, right_side)), own_mask(filters[2 * round_index])
         )

time: 891 us -> 861 us (0.966)
  waiting for transfers between devices: 771 us -> 733 us
    ppermute x0 -> x4, waiting for transfers between devices: none -> 98.4 us  [collect(): theirs = lax.ppermute(grown, axis, [(d, d ^ reach) for d in range(ways)])]
    all_gather x2 -> x0, waiting for transfers between devices: 70.4 us -> none  [on_device(): lax.all_gather(operand, 'depth', axis=1, tiled=True)]
    all_gather x4, waiting for transfers between devices: 127 us -> 66.3 us  [multiply(): lax.all_gather(left_tile, 'col', axis=1, tiled=True)]
  transfers between devices with their start and end apart: 12 -> 14, of which waited for: 12 -> 12; matrix products, arithmetic and copies ran while one was open for 4% -> 4% of each run, Pallas kernels for 0% -> 0%
where the time goes in v1:
time: 861 us; the launch traced here: 860 us
  waiting for transfers between devices  733 us (85%)
  matrix products  42.3 us (5%)
  local copies, waits for them, and re-layouts  34.7 us (4%)
  other arithmetic  30.2 us (4%)
  between operations  15.1 us (2%)
    psum x2, waiting for transfers between devices, spread(): return lax.psum(jnp.where(mine, value, jnp.zeros_like(value)), axis)  311 us
    reduce_scatter x4, waiting for transfers between devices, share_layers(): lax.psum_scatter(partial_sum, 'depth', scatter_dimension=1, tiled=True)  257 us
    ppermute x4, waiting for transfers between devices, collect(): theirs = lax.ppermute(grown, axis, [(d, d ^ reach) for d in range(ways)])  98.4 us
    all_gather x4, waiting for transfers between devices, multiply(): lax.all_gather(left_tile, 'col', axis=1, tiled=True)  66.3 us
    dot_general x4, matrix products, multiply(): jnp.dot(lax.all_gather(left_tile, 'col', axis=1, tiled=True), right_side,...  42.3 us
    mul x10, local copies, waits for them, and re-layouts, apply_mask(): values.reshape(row_count, BLK, col_count, BLK) * keep_mask[:, None, :, None]  32.3 us
  transfers between devices with their start and end apart: 14, of which 12 were waited for; matrix products, arithmetic and copies ran while one was open for 4% of the time, Pallas kernels for 0%

profile of v1, /device:TPU:0, one launch (start us, length us, event | category | flops | bytes accessed | tf_op | source)
XLA Modules:
  0.0 860.1 jit_solution(1468699436418513954)
XLA Ops:
  7.4 0.8 copy-done
  8.1 0.1 copy.14
  8.2 0.1 copy.5
  8.3 2.3 mul.83
  10.6 3.4 mul.84
  14.0 1.9 multiply_convert_fusion
  16.0 0.5 collective-permute-start
  16.5 2.4 collective-permute-done
  18.9 2.3 maximum_select_fusion.2
  21.2 2.9 collective-permute-start.1
  24.2 0.0 all-reduce.3.cloned.1.call-start
  24.2 46.0 %collective-permute-done.1 = bf16[1024,1024]{1,0:T(8,128)(2,1)} collective-permute-done((bf16[1024,1024]{1,0:T(8,128)(2,1)S(1)}, bf16[1024,1024]{1,0:T(8,128)(2,1)}, u32[]{:S(2)}, u32[]{:S(2)}) %collective-permute-start.1) | collective-permute-done | bytes 2097184 | tf_op jit(solution)/shard_map/ppermute | solution.py:14
  70.2 5.2 fusion
  75.4 0.0 all-reduce.3.cloned.1.call-update
  75.4 0.0 reduce-scatter.5.cloned.1.call-start
  75.4 0.0 all-gather.5.cloned.1.call-done
  75.5 156.3 %all-reduce.3.cloned.1.call-done = bf16[1024,2048]{1,0:T(8,128)(2,1)} async-done(((bf16[1024,2048]{1,0:T(8,128)(2,1)}), bf16[1024,2048]{1,0:T(8,128)(2,1)}) %all-reduce.3.cloned.1.call-update) | async-done | bytes 4194320 | tf_op jit(solution)/shard_map/psum | solution.py:24
  231.8 10.6 %fusion.3 = f32[1024,2048]{1,0:T(8,128)} fusion(bf16[1024,1024]{1,0:T(8,128)(2,1)} %all-gather.5.cloned.1.call-done, bf16[1024,2048]{1,0:T(8,128)(2,1)} %all-reduce.3.cloned.1.call-done), kind=kOutput, calls=%fused_computation.27 | convolution fusion | flops 4294967296 | bytes 14680064 | tf_op jit(solution)/shard_map/dot_general | solution.py:54
  242.4 0.0 all-gather.7.cloned.1.call-start
  242.4 0.8 copy-done.4
  243.3 0.1 copy.16
  243.4 0.1 copy.7
  243.4 2.3 mul.86
  245.7 3.8 mul.87
  249.5 63.7 %reduce-scatter.5.cloned.1.call-done = f32[1024,512]{1,0:T(8,128)} async-done(((f32[1024,2048]{1,0:T(8,128)}), f32[1024,512]{1,0:T(8,128)}) %reduce-scatter.5.cloned.1.call-update) | async-done | bytes 2097168 | tf_op jit(solution)/shard_map/reduce_scatter | solution.py:61
  313.2 2.9 multiply_convert_fusion.2
  316.2 0.0 reduce-scatter.7.cloned.1.call-start
  316.2 33.2 %all-gather.7.cloned.1.call-done = bf16[1024,1024]{1,0:T(8,128)(2,1)} async-done(((bf16[1024,512]{1,0:T(8,128)(2,1)}), bf16[1024,1024]{1,0:T(8,128)(2,1)}) %all-gather.7.cloned.1.call-update) | async-done | bytes 2097168 | tf_op jit(solution)/shard_map/all_gather | solution.py:55
  349.5 10.6 %fusion.4 = f32[1024,2048]{1,0:T(8,128)} fusion(bf16[1024,1024]{1,0:T(8,128)(2,1)} %all-gather.7.cloned.1.call-done, bf16[1024,2048]{1,0:T(8,128)(2,1)} %all-reduce.3.cloned.1.call-done), kind=kOutput, calls=%fused_computation.28 | convolution fusion | flops 4294967296 | bytes 14680064 | tf_op jit(solution)/shard_map/dot_general | solution.py:54
  360.0 0.2 all-gather.9.cloned.1.call-start
  360.3 0.1 copy.18
  360.4 0.1 copy.9
  360.5 2.3 mul.90
  362.8 5.0 mul.91
  367.8 64.1 %reduce-scatter.7.cloned.1.call-done = f32[1024,512]{1,0:T(8,128)} async-done(((f32[1024,2048]{1,0:T(8,128)}), f32[1024,512]{1,0:T(8,128)}) %reduce-scatter.7.cloned.1.call-update) | async-done | bytes 2097168 | tf_op jit(solution)/shard_map/reduce_scatter | solution.py:61
  432.0 3.9 subtract_convert_fusion
  435.9 0.1 collective-permute-start.2
  436.0 2.6 collective-permute-done.2
  438.6 0.6 maximum_select_fusion.3
  439.3 0.4 collective-permute-start.3
  439.7 0.0 all-reduce.5.cloned.1.call-start
  439.7 47.4 %collective-permute-done.3 = bf16[1024,1024]{1,0:T(8,128)(2,1)} collective-permute-done((bf16[1024,1024]{1,0:T(8,128)(2,1)S(1)}, bf16[1024,1024]{1,0:T(8,128)(2,1)}, u32[]{:S(2)}, u32[]{:S(2)}) %collective-permute-start.3) | collective-permute-done | bytes 2097184 | tf_op jit(solution)/shard_map/ppermute | solution.py:14
  487.1 5.2 fusion.1
  492.3 0.0 all-reduce.5.cloned.1.call-update
  492.3 0.0 reduce-scatter.9.cloned.1.call-start
  492.4 0.0 all-gather.9.cloned.1.call-done
  492.4 154.8 %all-reduce.5.cloned.1.call-done = bf16[1024,2048]{1,0:T(8,128)(2,1)} async-done(((bf16[1024,2048]{1,0:T(8,128)(2,1)}), bf16[1024,2048]{1,0:T(8,128)(2,1)}) %all-reduce.5.cloned.1.call-update) | async-done | bytes 4194320 | tf_op jit(solution)/shard_map/psum | solution.py:24
  647.2 10.6 %fusion.5 = f32[1024,2048]{1,0:T(8,128)} fusion(bf16[1024,1024]{1,0:T(8,128)(2,1)} %all-gather.9.cloned.1.call-done, bf16[1024,2048]{1,0:T(8,128)(2,1)} %all-reduce.5.cloned.1.call-done), kind=kOutput, calls=%fused_computation.29 | convolution fusion | flops 4294967296 | bytes 14680064 | tf_op jit(solution)/shard_map/dot_general | solution.py:54
  657.8 0.0 all-gather.11.cloned.1.call-start
  657.9 0.1 copy.20
  658.0 0.1 copy.11
  658.1 2.3 mul.94
  660.4 3.5 mul.95
  663.9 64.9 %reduce-scatter.9.cloned.1.call-done = f32[1024,512]{1,0:T(8,128)} async-done(((f32[1024,2048]{1,0:T(8,128)}), f32[1024,512]{1,0:T(8,128)}) %reduce-scatter.9.cloned.1.call-update) | async-done | bytes 2097168 | tf_op jit(solution)/shard_map/reduce_scatter | solution.py:61
  728.7 2.9 multiply_convert_fusion.1
  731.7 0.3 reduce-scatter.11.cloned.1.call-start
  732.0 33.0 %all-gather.11.cloned.1.call-done = bf16[1024,1024]{1,0:T(8,128)(2,1)} async-done(((bf16[1024,512]{1,0:T(8,128)(2,1)}), bf16[1024,1024]{1,0:T(8,128)(2,1)}) %all-gather.11.cloned.1.call-update) | async-done | bytes 2097168 | tf_op jit(solution)/shard_map/all_gather | solution.py:55
  765.0 10.6 %fusion.6 = f32[1024,2048]{1,0:T(8,128)} fusion(bf16[1024,1024]{1,0:T(8,128)(2,1)} %all-gather.11.cloned.1.call-done, bf16[1024,2048]{1,0:T(8,128)(2,1)} %all-reduce.5.cloned.1.call-done), kind=kOutput, calls=%fused_computation.30 | convolution fusion | flops 4294967296 | bytes 14680064 | tf_op jit(solution)/shard_map/dot_general | solution.py:54
  775.5 0.1 copy.22
  775.7 0.1 copy.13
  775.7 2.3 mul.98
  778.1 5.0 mul.99
  783.0 64.4 %reduce-scatter.11.cloned.1.call-done = f32[1024,512]{1,0:T(8,128)} async-done(((f32[1024,2048]{1,0:T(8,128)}), f32[1024,512]{1,0:T(8,128)}) %reduce-scatter.11.cloned.1.call-update) | async-done | bytes 2097168 | tf_op jit(solution)/shard_map/reduce_scatter | solution.py:61
  847.4 5.2 multiply_subtract_fusion
  (31 shorter events, 0.3 us)
Async XLA Ops:
  7.4 0.8 copy-start
  7.4 68.1 %all-gather.5.cloned.1.call-start = ((), (), s32[]{:S(2)}) async-start(), calls=%async_computation.4 | async-start | bytes 3145728 | tf_op jit(solution)/shard_map/all_gather | solution.py:55
  16.0 5.2 copy-start.2
  16.0 2.9 collective-permute-start
  21.2 49.0 %collective-permute-start.1 = (bf16[1024,1024]{1,0:T(8,128)(2,1)S(1)}, bf16[1024,1024]{1,0:T(8,128)(2,1)}, u32[]{:S(2)}, u32[]{:S(2)}) collective-permute-start(bf16[1024,1024]{1,0:T(8,128)(2,1)S(1)} %maximum_select_fusion.2), channel_id=1, source_target_pairs={{0,16},{8,24},{16,0},{24,8},{1,17},{9,25},{17,1},{25,9},{2,18},{10... | collective-permute-start | bytes 6291464 | tf_op jit(solution)/shard_map/ppermute | solution.py:14
  24.2 207.6 %all-reduce.3.cloned.1.call-start = ((), (), s32[]{:S(2)}) async-start(), calls=%async_computation.5 | async-start | bytes 8388608 | tf_op jit(solution)/shard_map/psum | solution.py:24
  75.4 237.9 %reduce-scatter.5.cloned.1.call-start = ((), (), s32[]{:S(2)}) async-start(), calls=%async_computation.6 | async-start | bytes 10485760 | tf_op jit(solution)/shard_map/reduce_scatter | solution.py:61
  242.3 0.9 copy-start.4
  242.4 107.1 %all-gather.7.cloned.1.call-start = ((), (), s32[]{:S(2)}) async-start(), calls=%async_computation.7 | async-start | bytes 3145728 | tf_op jit(solution)/shard_map/all_gather | solution.py:55
  316.2 115.8 %reduce-scatter.7.cloned.1.call-start = ((), (), s32[]{:S(2)}) async-start(), calls=%async_computation.8 | async-start | bytes 10485760 | tf_op jit(solution)/shard_map/reduce_scatter | solution.py:61
  360.0 132.4 %all-gather.9.cloned.1.call-start = ((), (), s32[]{:S(2)}) async-start(), calls=%async_computation.9 | async-start | bytes 3145728 | tf_op jit(solution)/shard_map/all_gather | solution.py:55
  435.9 3.4 copy-start.3
  435.9 2.7 collective-permute-start.2
  439.3 47.8 %collective-permute-start.3 = (bf16[1024,1024]{1,0:T(8,128)(2,1)S(1)}, bf16[1024,1024]{1,0:T(8,128)(2,1)}, u32[]{:S(2)}, u32[]{:S(2)}) collective-permute-start(bf16[1024,1024]{1,0:T(8,128)(2,1)S(1)} %maximum_select_fusion.3), channel_id=1, source_target_pairs={{0,16},{8,24},{16,0},{24,8},{1,17},{9,25},{17,1},{25,9},{2,18},{10... | collective-permute-start | bytes 6291464 | tf_op jit(solution)/shard_map/ppermute | solution.py:14
  439.7 207.5 %all-reduce.5.cloned.1.call-start = ((), (), s32[]{:S(2)}) async-start(), calls=%async_computation.10 | async-start | bytes 8388608 | tf_op jit(solution)/shard_map/psum | solution.py:24
  492.3 236.4 %reduce-scatter.9.cloned.1.call-start = ((), (), s32[]{:S(2)}) async-start(), calls=%async_computation.11 | async-start | bytes 10485760 | tf_op jit(solution)/shard_map/reduce_scatter | solution.py:61
  657.8 107.1 %all-gather.11.cloned.1.call-start = ((), (), s32[]{:S(2)}) async-start(), calls=%async_computation.12 | async-start | bytes 3145728 | tf_op jit(solution)/shard_map/all_gather | solution.py:55
  731.7 115.8 %reduce-scatter.11.cloned.1.call-start = ((), (), s32[]{:S(2)}) async-start(), calls=%async_computation.13 | async-start | bytes 10485760 | tf_op jit(solution)/shard_map/reduce_scatter | solution.py:61
  847.4 5.2 copy-start.1
Sparse Core Ops, SparseCore 0:
  24.3 33.4 all-gather.4
  242.5 70.7 reduce-scatter.4
  316.3 33.1 all-gather.6
  360.2 71.7 reduce-scatter.6
  439.8 34.2 all-gather.8
  657.9 70.7 reduce-scatter.8
  731.8 33.1 all-gather.10
  775.7 71.7 reduce-scatter.10
Sparse Core Ops, SparseCore 1:
  75.5 156.2 all-reduce.2
  492.4 154.8 all-reduce.4
